TPU v7x, 32 devices: a whole 2x2x4 slice. The times are simulated.
32 devices in a mesh: groups: 2 (over x), gx: 2 (over core), gy: 8 (over z, y).
Axes of the slice: x: 2, y: 2, z: 4, core: 2. Of those that a mesh axis runs over, the one named last changes fastest.
Arguments:
- inputs: bfloat16 [24, 16384], P('groups', ('gx', 'gy')), parts along dimension 0, may hold values from -6 to 6
- norm_gain: bfloat16 [16384], P(('gx', 'gy')), may hold values from 0.099609375 to 1.8984375
- w_query: bfloat16 [16384, 8192], P('gx', 'gy'), may hold values from -0.046875 to 0.046875
- w_key: bfloat16 [16384, 512], P('gx', 'gy'), may hold values from -0.046875 to 0.046875
- w_value: bfloat16 [16384, 512], P('gx', 'gy'), may hold values from -0.046875 to 0.046875
- w_out: bfloat16 [8192, 16384], P('gy', 'gx'), may hold values from -0.25 to 0.25
- key_cache: bfloat16 [24, 16384, 128], P(('groups', 'gx'), 'gy'), parts along dimension 0, may hold values from -480 to 480
- value_cache: bfloat16 [24, 16384, 128], P(('groups', 'gx'), 'gy'), parts along dimension 0, may hold values from -6 to 6
- lengths: int32 [24], P(('groups', 'gx')), parts along dimension 0, may hold values from 1 to 4096, as said below
Outputs:
- output: bfloat16 [24, 16384], P('groups', ('gx', 'gy')), parts along dimension 0
There are 2 independent parts, one for each index of `groups`. A program takes and returns all parts, laid end to end along the dimension named above; an argument that names none is the same for every part. Nothing has to cross between parts.
Inputs may be any that keep to these rules, and one draw needn't show every extreme that they name: `lengths`: one row has exactly 4096 cached tokens and another exactly 1.
All inputs are finite; a program needn't handle non-finite values.
Results may differ from a plain program's by a relative error of at most 0.017.
Values may be sent and summed in bfloat16 or wider, within the bound.
A program may use at most 128 MiB of HBM per device.

v0:
```python
import jax
import jax.numpy as jnp
from jax import lax
from jax.sharding import PartitionSpec as P

D = 16384
HQ = 64
KVH = 4
HD = 128


huge_score = 1e30


def rotate(values, where_at):
    half_dim = values.shape[-1] // 2
    freq_index = jnp.arange(half_dim, dtype=jnp.float32)
    inverse = 500000.0 ** (-2.0 * freq_index / values.shape[-1])
    angles = where_at.astype(jnp.float32)[:, None] * inverse[None, :]
    cosine = jnp.cos(angles)[:, None, :]
    sine_part = jnp.sin(angles)[:, None, :]
    front_half = values[..., :half_dim]
    back_half = values[..., half_dim:]
    return jnp.concatenate(
        [front_half * cosine - back_half * sine_part, back_half * cosine + front_half * sine_part],
        axis=-1,
    )


def partial_attention(
    query_block, key_block, value_block, own_key, own_value, live_mask, with_self
):
    score_scale = query_block.shape[-1] ** (-0.5)
    scores = (
        jnp.einsum("rgd,rtd->rgt", query_block, key_block, preferred_element_type=jnp.float32)
        * score_scale
    )
    self_score = (
        jnp.sum(query_block.astype(jnp.float32) * own_key.astype(jnp.float32)[:, None, :], axis=-1)
        * score_scale
    )
    masked = jnp.where(live_mask[:, None, :], scores, -huge_score)
    self_live = jnp.where(with_self, self_score, -huge_score)
    best_score = jnp.maximum(jnp.max(masked, axis=-1), self_live)
    exp_weights = jnp.where(live_mask[:, None, :], jnp.exp(masked - best_score[..., None]), 0.0)
    self_weight = jnp.where(with_self, jnp.exp(self_live - best_score), 0.0)
    denominator = jnp.sum(exp_weights, axis=-1) + self_weight
    weighted = jnp.einsum(
        "rgt,rtd->rgd",
        exp_weights.astype(jnp.bfloat16),
        value_block,
        preferred_element_type=jnp.float32,
    )
    weighted = (
        weighted
        + self_weight.astype(jnp.bfloat16).astype(jnp.float32)[..., None]
        * own_value.astype(jnp.float32)[:, None, :]
    )
    return (best_score, denominator, weighted)


def spread_heads(values, group_index, fill_value):
    shape_rest = values.shape[2:]
    filled = jnp.full((values.shape[0], values.shape[1], KVH) + shape_rest, fill_value, jnp.float32)
    placed = lax.dynamic_update_slice_in_dim(filled, values[:, :, None], group_index, 2)
    return placed.reshape((values.shape[0], values.shape[1] * KVH) + shape_rest)


def pick_heads(values, group_index):
    shape_rest = values.shape[2:]
    grouped = values.reshape((values.shape[0], values.shape[1] // KVH, KVH) + shape_rest)
    return lax.dynamic_index_in_dim(grouped, group_index, 2, keepdims=False)


def local(inputs, norm_gain, w_query, w_key, w_value, w_out, key_cache, value_cache, lengths):
    gathered, gain_half = (
        lax.all_gather(inputs, "gy", axis=1, tiled=True),
        lax.all_gather(norm_gain, "gy", axis=0, tiled=True),
    )
    floats = gathered.astype(jnp.float32)
    squares = lax.psum(jnp.sum(floats * floats, axis=-1), "gx")
    scale_inv = lax.rsqrt(squares[:, None] / D + 1e-05)
    normed = (floats * scale_inv * gain_half.astype(jnp.float32)).astype(jnp.bfloat16)
    query_part = jnp.dot(normed, w_query, preferred_element_type=jnp.float32)
    key_part = jnp.dot(normed, w_key, preferred_element_type=jnp.float32)
    value_part = jnp.dot(normed, w_value, preferred_element_type=jnp.float32)
    query_sum, key_sum, value_sum = (
        lax.psum_scatter(query_part, "gx", scatter_dimension=0, tiled=True),
        lax.psum_scatter(key_part, "gx", scatter_dimension=0, tiled=True),
        lax.psum_scatter(value_part, "gx", scatter_dimension=0, tiled=True),
    )
    half_rows = query_sum.shape[0]
    heads_here = query_sum.shape[1] // HD
    count_gy = lax.axis_size("gy")
    blocks_per_head = count_gy // KVH
    device_index = lax.axis_index("gy")
    group_index = device_index // blocks_per_head
    block_index = device_index % blocks_per_head
    own_queries = rotate(query_sum.reshape(half_rows, heads_here, HD), lengths).astype(jnp.bfloat16)
    all_queries = lax.all_gather(
        own_queries.reshape(half_rows, heads_here * HD), "gy", axis=1, tiled=True
    )
    all_keys, all_values = (
        lax.all_gather(key_sum, "gy", axis=1, tiled=True),
        lax.all_gather(value_sum, "gy", axis=1, tiled=True),
    )
    query_block = pick_heads(all_queries.reshape(half_rows, HQ, HD), group_index)
    key_raw = lax.dynamic_index_in_dim(
        all_keys.reshape(half_rows, HD, KVH), group_index, 2, keepdims=False
    )
    own_key = (
        rotate(key_raw.reshape(half_rows, 1, HD), lengths)
        .astype(jnp.bfloat16)
        .reshape(half_rows, HD)
    )
    own_value = lax.dynamic_index_in_dim(
        all_values.reshape(half_rows, HD, KVH), group_index, 2, keepdims=False
    ).astype(jnp.bfloat16)
    span_len = key_cache.shape[1]
    positions = block_index * span_len + jnp.arange(span_len, dtype=jnp.int32)
    live_mask = positions[None, :] < lengths[:, None]
    best_score, denominator, weighted = partial_attention(
        query_block, key_cache, value_cache, own_key, own_value, live_mask, block_index == 0
    )
    full_best = spread_heads(best_score, group_index, -huge_score).reshape(
        half_rows, count_gy, heads_here
    )
    full_denom = spread_heads(denominator, group_index, 0.0).reshape(
        half_rows, count_gy, heads_here
    )
    full_weighted = spread_heads(weighted, group_index, 0.0).reshape(
        half_rows, count_gy, heads_here, HD
    )
    send_best = jnp.transpose(full_best, (1, 0, 2))
    send_denom = jnp.transpose(full_denom, (1, 0, 2))
    send_weighted = jnp.transpose(full_weighted, (1, 0, 2, 3))
    received = (
        lax.all_to_all(send_best, "gy", split_axis=0, concat_axis=0, tiled=True),
        lax.all_to_all(send_denom, "gy", split_axis=0, concat_axis=0, tiled=True),
        lax.all_to_all(send_weighted, "gy", split_axis=0, concat_axis=0, tiled=True),
    )
    overall = jnp.max(received[0], axis=0)
    factor = jnp.exp(received[0] - overall[None])
    denom_mine = jnp.sum(factor * received[1], axis=0)
    weighted_mine = jnp.sum(factor[..., None] * received[2], axis=0)
    attended = (
        (weighted_mine / denom_mine[..., None])
        .reshape(half_rows, heads_here * HD)
        .astype(jnp.bfloat16)
    )
    partial_out = jnp.dot(
        lax.all_gather(attended, "gx", axis=0, tiled=True),
        w_out,
        preferred_element_type=jnp.float32,
    )
    return lax.psum_scatter(partial_out.astype(jnp.bfloat16), "gy", scatter_dimension=1, tiled=True)


def solution(mesh):
    placed = (
        P("groups", ("gx", "gy")),
        P(("gx", "gy")),
        P("gx", "gy"),
        P("gx", "gy"),
        P("gx", "gy"),
        P("gy", "gx"),
        P(("groups", "gx"), "gy", None),
        P(("groups", "gx"), "gy", None),
        P(("groups", "gx")),
    )
    return jax.shard_map(
        local, mesh=mesh, in_specs=placed, out_specs=P("groups", ("gx", "gy")), check_vma=False
    )
```

profile of v0, /device:TPU:0, one launch (start us, length us, event | category | flops | bytes accessed | tf_op | source)
XLA Modules:
  0.0 302.5 jit_solution(5637722720923297889)
XLA Ops:
  6.5 32.9 %all_gather.18 = bf16[12,8192]{1,0:T(8,128)(2,1)S(1)} all-gather(bf16[12,1024]{1,0:T(8,128)(2,1)} %param.9), channel_id=1, replica_groups=mesh['groups'=2,'gx'=2,'gy'=8] {'gy'}, dimensions={1}, use_global_device_ids=true | all-gather | bytes 221184 | tf_op jit(solution)/shard_map/all_gather | solution.py:77
  39.6 2.5 psum.7
  42.1 26.1 %all_gather.19 = bf16[8192]{0:T(1024)(128)(2,1)S(1)} all-gather(bf16[1024]{0:T(1024)(128)(2,1)} %param.10), channel_id=1, replica_groups=mesh['groups'=2,'gx'=2,'gy'=8] {'gy'}, dimensions={0}, use_global_device_ids=true | all-gather | bytes 18432 | tf_op jit(solution)/shard_map/all_gather | solution.py:78
  68.2 8.1 %fusion.22 = f32[12,1024]{1,0:T(8,128)S(1)} fusion(bf16[8192,1024]{1,0:T(8,128)(2,1)} %param.11, bf16[12,8192]{1,0:T(8,128)(2,1)S(1)} %all_gather.18, f32[8192]{0:T(1024)S(1)} %convert_element_type.81, f32[12]{0:T(128)S(1)} %add_rsqrt_fusion), kind=kOutput, calls=%fused_computation.59 | convolution fusion | flops 201719808 | bytes 17055792 | tf_op jit(solution)/shard_map/dot_general | solution.py:84
  76.3 2.9 fusion
  79.8 2.8 collective-permute-start
  83.2 1.6 fusion.18
  84.8 1.7 fusion.20
  86.5 3.9 %all-reduce.4 = (f32[12,64]{1,0:T(8,128)S(1)}, bf16[12,64]{1,0:T(8,128)(2,1)}) all-reduce(f32[12,64]{1,0:T(8,128)S(1)} %fusion.20, f32[12,64]{1,0:T(8,128)S(1)} %fusion.18), channel_id=3, replica_groups=mesh['groups'=2,'gx'=2,'gy'=8] {'gx'}, use_global_device_ids=true, to_apply=%region_4.0.clone | all-reduce | flops 1536 | bytes 10752
  91.6 30.4 %all-gather = f32[8,64,6]{1,2,0:T(8,128)S(1)} all-gather(f32[1,64,6]{1,2,0:T(8,128)S(1)} %dynamic-slice_bitcast_fusion.2), channel_id=1, replica_groups=mesh['groups'=2,'gx'=2,'gy'=8] {'gy'}, dimensions={0}, use_global_device_ids=true | all-gather | bytes 13824 | tf_op jit(solution)/shard_map/all_gather | solution.py:104
  123.5 0.8 multiply_cosine_fusion
  124.3 0.8 subtract_convert_fusion.1
  127.3 26.0 %all-gather.1 = bf16[8,64,6]{1,2,0:T(8,128)(2,1)S(1)} all-gather(bf16[1,64,6]{1,2,0:T(8,128)(2,1)S(1)} %dynamic-slice_bitcast_fusion.1), channel_id=1, replica_groups=mesh['groups'=2,'gx'=2,'gy'=8] {'gy'}, dimensions={0}, use_global_device_ids=true | all-gather | bytes 6912 | tf_op jit(solution)/shard_map/all_gather | solution.py:105
  153.8 1.6 concatenate.23
  155.6 30.7 %all_gather.20 = bf16[6,8192]{1,0:T(8,128)(2,1)S(1)} all-gather(bf16[6,1024]{1,0:T(8,128)(2,1)S(1)} %bitcast.76), channel_id=1, replica_groups=mesh['groups'=2,'gx'=2,'gy'=8] {'gy'}, dimensions={1}, use_global_device_ids=true | all-gather | bytes 110592 | tf_op jit(solution)/shard_map/all_gather | solution.py:100
  186.3 0.8 reshape_reshape.12
  187.1 0.9 constant_dynamic-slice_fusion
  188.2 1.0 fusion.25
  189.2 0.9 copy-done.1
  191.1 1.4 dynamic_update_slice.9
  192.5 3.3 %all-to-all-start = ((f32[8,6,8]{1,2,0:T(8,128)}), f32[8,6,8]{1,2,0:T(8,128)S(1)}, u32[]{:S(2)}, u32[]{:S(2)}) async-start(f32[8,6,8]{1,2,0:T(8,128)} %bitcast.6), calls=%async_computation | async-start | bytes 65536 | tf_op jit(solution)/shard_map/all_to_all | solution.py:138
  196.8 1.4 dynamic_update_slice.11
  198.2 4.3 %all-to-all-done = f32[8,6,8]{1,2,0:T(8,128)S(1)} async-done(((f32[8,6,8]{1,2,0:T(8,128)}), f32[8,6,8]{1,2,0:T(8,128)S(1)}, u32[]{:S(2)}, u32[]{:S(2)}) %all-to-all-start) | async-done | bytes 1568 | tf_op jit(solution)/shard_map/all_to_all | solution.py:138
  202.5 3.3 %all-to-all-start.2 = ((f32[8,6,8]{1,2,0:T(8,128)}), f32[8,6,8]{1,2,0:T(8,128)S(1)}, u32[]{:S(2)}, u32[]{:S(2)}) async-start(f32[8,6,8]{1,2,0:T(8,128)} %bitcast.16), calls=%async_computation.2 | async-start | bytes 65536 | tf_op jit(solution)/shard_map/all_to_all | solution.py:139
  205.8 2.7 convolution_add_fusion
  208.6 1.8 dynamic_update_slice.10
  211.1 1.3 all-to-all-done.2
  212.4 4.6 %all-to-all-start.1 = ((f32[8,6,8,128]{3,2,1,0:T(8,128)}), f32[8,6,8,128]{3,2,1,0:T(8,128)S(1)}, u32[]{:S(2)}, u32[]{:S(2)}) async-start(f32[8,6,8,128]{3,2,1,0:T(8,128)} %copy.44), calls=%async_computation.1 | async-start | bytes 393216 | tf_op jit(solution)/shard_map/all_to_all | solution.py:140
  217.4 7.5 %all-to-all-done.1 = f32[8,6,8,128]{3,2,1,0:T(8,128)S(1)} async-done(((f32[8,6,8,128]{3,2,1,0:T(8,128)}), f32[8,6,8,128]{3,2,1,0:T(8,128)S(1)}, u32[]{:S(2)}, u32[]{:S(2)}) %all-to-all-start.1) | async-done | bytes 196640 | tf_op jit(solution)/shard_map/all_to_all | solution.py:140
  225.1 1.8 all-gather.2
  227.0 8.8 %convolution_convert_fusion = bf16[12,8192]{1,0:T(8,128)(2,1)} fusion(bf16[12,1024]{1,0:T(8,128)(2,1)S(1)} %reshape.253, bf16[1024,8192]{1,0:T(8,128)(2,1)} %param.14), kind=kOutput, calls=%fused_computation | convolution fusion | flops 201424896 | bytes 16998400 | tf_op jit(solution)/shard_map/dot_general | solution.py:151
  235.7 59.9 %reduce-scatter.4.cloned.1.call-done = bf16[12,1024]{1,0:T(8,128)(2,1)} async-done(((bf16[12,8192]{1,0:T(8,128)(2,1)}), bf16[12,1024]{1,0:T(8,128)(2,1)}) %reduce-scatter.4.cloned.1.call-update) | async-done | bytes 24592 | tf_op jit(solution)/shard_map/reduce_scatter | solution.py:156
  (55 shorter events, 9.0 us)
Async XLA Ops:
  6.5 181.6 %copy-start = (bf16[6,2048,128]{2,1,0:T(8,128)(2,1)S(1)}, bf16[6,2048,128]{2,1,0:T(8,128)(2,1)}, u32[]{:S(2)}) copy-start(bf16[6,2048,128]{2,1,0:T(8,128)(2,1)} %param.15) | copy-start | bytes 9437188
  6.5 83.8 %copy-start.3 = (u32[32]{0:T(128)S(1)}, u32[32]{0:T(128)}, u32[]{:S(2)}) copy-start(u32[32]{0:T(128)} %constant.72) | copy-start | bytes 388
  79.2 43.0 %copy-start.2 = (f32[8,1024]{1,0:T(8,128)}, f32[8,1024]{1,0:T(8,128)S(1)}, u32[]{:S(2)}) copy-start(f32[8,1024]{1,0:T(8,128)S(1)} %fusion) | copy-start | bytes 98308
  79.8 74.1 %collective-permute-start = (f32[2,1024]{1,0:T(2,128)}, f32[2,1024]{1,0:T(2,128)}, u32[]{:S(2)}, u32[]{:S(2)}) collective-permute-start(f32[2,1024]{1,0:T(2,128)} %slice.20), channel_id=1, source_target_pairs={{0,8},{1,9},{2,10},{3,11},{4,12},{5,13},{6,14},{7,15},{16,24},{17,... | collective-permute-start | bytes 24584
  189.2 0.9 copy-start.1
  192.5 10.0 %all-to-all-start = ((f32[8,6,8]{1,2,0:T(8,128)}), f32[8,6,8]{1,2,0:T(8,128)S(1)}, u32[]{:S(2)}, u32[]{:S(2)}) async-start(f32[8,6,8]{1,2,0:T(8,128)} %bitcast.6), calls=%async_computation | async-start | bytes 65536 | tf_op jit(solution)/shard_map/all_to_all | solution.py:138
  202.5 10.0 %all-to-all-start.2 = ((f32[8,6,8]{1,2,0:T(8,128)}), f32[8,6,8]{1,2,0:T(8,128)S(1)}, u32[]{:S(2)}, u32[]{:S(2)}) async-start(f32[8,6,8]{1,2,0:T(8,128)} %bitcast.16), calls=%async_computation.2 | async-start | bytes 65536 | tf_op jit(solution)/shard_map/all_to_all | solution.py:139
  212.4 12.4 %all-to-all-start.1 = ((f32[8,6,8,128]{3,2,1,0:T(8,128)}), f32[8,6,8,128]{3,2,1,0:T(8,128)S(1)}, u32[]{:S(2)}, u32[]{:S(2)}) async-start(f32[8,6,8,128]{3,2,1,0:T(8,128)} %copy.44), calls=%async_computation.1 | async-start | bytes 393216 | tf_op jit(solution)/shard_map/all_to_all | solution.py:140
  217.1 78.6 %reduce-scatter.4.cloned.1.call-start = ((), (), s32[]{:S(2)}) async-start(), calls=%async_computation.4 | async-start | bytes 294912 | tf_op jit(solution)/shard_map/reduce_scatter | solution.py:156
Sparse Core Ops, SparseCore 0:
  235.9 59.7 reduce-scatter.3
where the time goes:
time: 304 us; the launch traced here: 303 us
  blocking collectives  157 us (52%)
  waiting for transfers between devices  73 us (24%)
  matrix products  23.9 us (8%)
  between operations  14.9 us (5%)
  local copies, waits for them, and re-layouts  14.5 us (5%)
  starting transfers between devices  14.2 us (5%)
  other arithmetic  4.91 us (2%)
    reduce_scatter x1, waiting for transfers between devices, local(): lax.psum_scatter(partial_out.astype(jnp.bfloat16), 'gy', scatter_dimensio...  59.9 us
    all_gather x1, blocking collectives, local(): lax.all_gather(inputs, 'gy', axis=1, tiled=True)  32.9 us
    all_gather x1, blocking collectives, local(): lax.all_gather(own_queries.reshape(half_rows, heads_here * HD), 'gy', axi...  30.7 us
    all_gather x1, blocking collectives, local(): lax.all_gather(key_sum, 'gy', axis=1, tiled=True)  30.4 us
    all_gather x1, blocking collectives, local(): lax.all_gather(norm_gain, 'gy', axis=0, tiled=True)  26.1 us
    all_gather x1, blocking collectives, local(): lax.all_gather(value_sum, 'gy', axis=1, tiled=True)  26 us
    dot_general x1, matrix products, local(): jnp.dot(lax.all_gather(attended, 'gx', axis=0, tiled=True), w_out, prefer...  8.76 us
    dot_general x1, matrix products, local(): query_part = jnp.dot(normed, w_query, preferred_element_type=jnp.float32)  8.08 us
  transfers between devices with their start and end apart: 5, of which 4 were waited for; matrix products, arithmetic and copies ran while one was open for 6% of the time, Pallas kernels for 0%

commit v1 on v0

v1 whole, which is shorter than its diff:
```python
import functools

import jax
import jax.numpy as jnp
from jax import lax
from jax.experimental import pallas as pl
from jax.experimental.pallas import tpu as pltpu
from jax.sharding import PartitionSpec as P

KVH = 4
HD = 128
SUB = 8
HUGE = 1e30
MESH = pl.DeviceIdType.MESH


def rope_table(lengths):
    half_dim = HD // 2
    freq_index = jnp.arange(half_dim, dtype=jnp.float32)
    inverse = 500000.0 ** (-2.0 * freq_index / HD)
    floats = lengths.astype(jnp.float32)
    angles = floats[:, None] * inverse[None, :]
    cosine, sine = jnp.cos(angles), jnp.sin(angles)
    table = jnp.stack(
        [
            jnp.concatenate([cosine, cosine], axis=1),
            jnp.concatenate([-sine, sine], axis=1),
            jnp.broadcast_to(floats[:, None], (lengths.shape[0], HD)),
        ]
    )
    return jnp.pad(table, ((0, 0), (0, SUB - lengths.shape[0]), (0, 0)))


def block_kernel(
    gy, gx_count, rows,
    table, xp, wq, wk, wv, wo, kc, vc,
    out,
    xall, ssq, wq_v, wk_v, wv_v, wo_v, kc_v, vc_v,
    part, kpart, vpart, part_in, qsend, qin, qg, outbox, inbox, att, osend, oin,
    sem_wq, sem_wk, sem_wv, sem_wo, sem_kc, sem_vc,
    ssq_s, ssq_r, x_s, x_r, part_s, part_r, q_s, q_r, box_s, box_r, att_s, att_r, o_s, o_r,
):
    gx = lax.axis_index("gx")
    me = lax.axis_index("gy")
    other = 1 - gx
    bd = xp.shape[1]
    qw = wq.shape[1]
    ck = wk.shape[1]
    span = kc.shape[1]
    ow = wo.shape[1] // gy
    hh = qw // HD
    hq = max(1, hh // KVH)
    nq = gy * hh // KVH
    bph = gy // KVH
    group = me // bph
    block = me % bph
    d_model = bd * gy * gx_count

    def load_in(step):
        base = pl.multiple_of(((me + step) % gy) * bd, bd)
        rows_here = pl.ds(base, bd)
        return (
            pltpu.make_async_copy(wq.at[rows_here, :], wq_v.at[step], sem_wq.at[step]),
            pltpu.make_async_copy(wk.at[rows_here, :], wk_v.at[step], sem_wk.at[step]),
            pltpu.make_async_copy(wv.at[rows_here, :], wv_v.at[step], sem_wv.at[step]),
        )

    def load_out(step):
        base = pl.multiple_of(((me + step) % gy) * ow, ow)
        return pltpu.make_async_copy(wo.at[:, pl.ds(base, ow)], wo_v.at[step], sem_wo.at[step])

    def load_cache(row):
        return (
            pltpu.make_async_copy(kc.at[row], kc_v.at[row], sem_kc.at[row]),
            pltpu.make_async_copy(vc.at[row], vc_v.at[row], sem_vc.at[row]),
        )

    for step in range(gy):
        for copy in load_in(step):
            copy.start()

    barrier = pltpu.get_barrier_semaphore()
    for side in range(gx_count):
        for step in range(gy):
            if side == 0 and step == 0:
                continue
            pl.semaphore_signal(
                barrier, inc=1,
                device_id={"gx": (gx + side) % gx_count, "gy": (me + step) % gy},
                device_id_type=MESH,
            )

    mine = xp[...].astype(jnp.float32)
    diagonal = lax.broadcasted_iota(jnp.int32, (2 * SUB, HD), 0) == lax.broadcasted_iota(
        jnp.int32, (2 * SUB, HD), 1
    )
    squares = jnp.sum(mine * mine, axis=1, keepdims=True)
    my_id = gx * gy + me
    ssq[my_id] = jnp.broadcast_to(
        jnp.sum(jnp.where(diagonal, squares, 0.0), axis=0, keepdims=True), (SUB, HD)
    )
    xall[me] = xp[...]

    pl.semaphore_wait(barrier, gx_count * gy - 1)

    def ssq_copy(side, step, source):
        return pltpu.make_async_remote_copy(
            src_ref=ssq.at[my_id, pl.ds(0, 1)], dst_ref=ssq.at[source, pl.ds(0, 1)],
            send_sem=ssq_s.at[side, step], recv_sem=ssq_r.at[source],
            device_id={"gx": (gx + side) % gx_count, "gy": (me + step) % gy},
            device_id_type=MESH,
        )

    def peer_copy(src, dst, send, recv, step):
        return pltpu.make_async_remote_copy(
            src_ref=src, dst_ref=dst, send_sem=send, recv_sem=recv,
            device_id={"gy": (me + step) % gy}, device_id_type=MESH,
        )

    def core_copy(src, dst, send, recv):
        return pltpu.make_async_remote_copy(
            src_ref=src, dst_ref=dst, send_sem=send, recv_sem=recv,
            device_id={"gx": other}, device_id_type=MESH,
        )

    def x_copy(step, source):
        return peer_copy(xp, xall.at[source], x_s.at[step], x_r.at[source], step)

    for side in range(gx_count):
        for step in range(gy):
            if side or step:
                ssq_copy(side, step, my_id).start()
    for step in range(1, gy):
        x_copy(step, me).start()
    for row in range(rows):
        for copy in load_cache(row):
            copy.start()

    part[...] = jnp.zeros_like(part)
    kpart[...] = jnp.zeros_like(kpart)
    vpart[...] = jnp.zeros_like(vpart)
    outbox[...] = jnp.zeros_like(outbox)

    for side in range(gx_count):
        for step in range(gy):
            if side or step:
                source = ((gx + side) % gx_count) * gy + (me + step) % gy
                ssq_copy(side, step, source).wait_recv()
    total = jnp.sum(ssq[:, 0, :], axis=0, keepdims=True)
    total = jnp.sum(jnp.where(diagonal, total, 0.0), axis=1, keepdims=True)
    scale_inv = lax.rsqrt(total / d_model + 1e-05)

    def project(step):
        source = (me + step) % gy
        features = xall[source].astype(jnp.float32)
        gain = features[rows : rows + 1, :]
        normed = (features * scale_inv * gain).astype(jnp.bfloat16)
        for copy in load_in(step):
            copy.wait()
        query = jnp.dot(normed, wq_v[step], preferred_element_type=jnp.float32)
        part[0, :, :qw] += query[:SUB]
        part[1, :, :qw] += query[SUB:]
        kpart[...] += jnp.dot(normed, wk_v[step], preferred_element_type=jnp.float32)
        vpart[...] += jnp.dot(normed, wv_v[step], preferred_element_type=jnp.float32)

    project(0)

    @pl.loop(1, gy)
    def _(step):
        source = (me + step) % gy
        x_copy(step, source).wait_recv()
        project(step)

    for side in range(2):
        part[side, :, qw : qw + ck] = kpart[side * SUB : (side + 1) * SUB]
        part[side, :, qw + HD : qw + HD + ck] = vpart[side * SUB : (side + 1) * SUB]

    swap = core_copy(part.at[other], part_in, part_s, part_r)
    swap.start()
    for step in range(gy):
        load_out((step + 1) % gy).start()
    column = lax.broadcasted_iota(jnp.int32, (HD, KVH * HD), 0)
    target = lax.broadcasted_iota(jnp.int32, (HD, KVH * HD), 1)
    wanted = (target % HD) * KVH + target // HD
    select = jnp.where((column < ck) & (column + me * ck == wanted), 1.0, 0.0).astype(jnp.bfloat16)
    cosine, sine, lens = table[0], table[1], table[2]
    swap.wait_recv()

    def rotated(values):
        return values * cosine + pltpu.roll(values, HD // 2, 1) * sine

    summed = part[gx] + part_in[...]
    for slot in range(hh):
        turned = rotated(summed[:, slot * HD : (slot + 1) * HD])
        to_group = slot % KVH if hh % KVH == 0 else (me * hh + slot) % KVH
        qsend[to_group, slot // KVH] = turned.astype(jnp.bfloat16).astype(jnp.float32)
    pair = jnp.concatenate([summed[:, qw : qw + HD], summed[:, qw + HD :]], axis=0)
    high = pair.astype(jnp.bfloat16)
    rest = pair - high.astype(jnp.float32)
    middle = rest.astype(jnp.bfloat16)
    low = (rest - middle.astype(jnp.float32)).astype(jnp.bfloat16)
    placed = (
        jnp.dot(high, select, preferred_element_type=jnp.float32)
        + jnp.dot(middle, select, preferred_element_type=jnp.float32)
        + jnp.dot(low, select, preferred_element_type=jnp.float32)
    )
    for g in range(KVH):
        qsend[g, hq] = placed[:SUB, g * HD : (g + 1) * HD]
        qsend[g, hq + 1] = placed[SUB:, g * HD : (g + 1) * HD]

    def q_copy(step, source):
        return peer_copy(
            qsend.at[((me + step) % gy) // bph], qin.at[source],
            q_s.at[step], q_r.at[source], step,
        )

    for step in range(1, gy):
        q_copy(step, me).start()
    qin[me] = qsend[group]
    for step in range(1, gy):
        q_copy(step, (me + step) % gy).wait_recv()

    for n in range(nq):
        if hh % KVH == 0:
            qg[n] = qin[n * KVH // hh, (n * KVH % hh) // KVH]
        else:
            qg[n] = qin[(n * KVH + group) // hh, 0]
    own_key = rotated(jnp.sum(qin[:, hq], axis=0)).astype(jnp.bfloat16).astype(jnp.float32)
    own_value = jnp.sum(qin[:, hq + 1], axis=0).astype(jnp.bfloat16).astype(jnp.float32)

    score_scale = HD ** (-0.5)
    with_self = (lax.broadcasted_iota(jnp.int32, (nq, 1), 0) * 0 + block) == 0
    positions = (lax.broadcasted_iota(jnp.int32, (nq, span), 1) + block * span).astype(jnp.float32)
    lane = lax.broadcasted_iota(jnp.int32, (nq, HD), 1)
    for row in range(rows):
        for copy in load_cache(row):
            copy.wait()
        query = qg[:, row, :]
        scores = (
            lax.dot_general(
                query.astype(jnp.bfloat16), kc_v[row], (((1,), (1,)), ((), ())),
                preferred_element_type=jnp.float32,
            )
            * score_scale
        )
        live = positions < lens[row : row + 1, 0:1]
        masked = jnp.where(live, scores, -HUGE)
        self_score = (
            jnp.sum(query * own_key[row : row + 1, :], axis=1, keepdims=True) * score_scale
        )
        self_live = jnp.where(with_self, self_score, -HUGE)
        best = jnp.maximum(jnp.max(masked, axis=1, keepdims=True), self_live)
        weights = jnp.where(live, jnp.exp(masked - best), 0.0)
        self_weight = jnp.where(with_self, jnp.exp(self_live - best), 0.0)
        denominator = jnp.sum(weights, axis=1, keepdims=True) + self_weight
        weighted = jnp.dot(
            weights.astype(jnp.bfloat16), vc_v[row], preferred_element_type=jnp.float32
        )
        weighted = (
            weighted
            + self_weight.astype(jnp.bfloat16).astype(jnp.float32) * own_value[row : row + 1, :]
        )
        outbox[:, 0, row, :] = weighted
        outbox[:, 1, row, :] = jnp.where(lane < HD // 2, best, denominator)

    def box_copy(step, source):
        first = (((me + step) % gy) * hh) // KVH
        return peer_copy(
            outbox.at[pl.ds(first, hq)], inbox.at[source], box_s.at[step], box_r.at[source], step
        )

    for step in range(1, gy):
        box_copy(step, me).start()
    inbox[me] = outbox[pl.ds((me * hh) // KVH, hq)]
    for step in range(1, gy):
        box_copy(step, (me + step) % gy).wait_recv()

    for slot in range(hh):
        of_group = slot % KVH if hh % KVH == 0 else (me * hh + slot) % KVH
        sums = [inbox[of_group * bph + b, slot // KVH, 0] for b in range(bph)]
        stats = [inbox[of_group * bph + b, slot // KVH, 1] for b in range(bph)]
        bests = [s[:, 0:1] for s in stats]
        denominators = [s[:, HD // 2 : HD // 2 + 1] for s in stats]
        overall = functools.reduce(jnp.maximum, bests)
        factors = [jnp.exp(b - overall) for b in bests]
        denominator = sum(f * d for f, d in zip(factors, denominators))
        weighted = sum(f * s for f, s in zip(factors, sums))
        att[gx, :, slot * HD : (slot + 1) * HD] = (
            (weighted / denominator).astype(jnp.bfloat16).astype(jnp.float32)
        )

    att_swap = core_copy(att.at[gx], att.at[gx], att_s, att_r)
    att_swap.start()
    core_copy(att.at[other], att.at[other], att_s, att_r).wait_recv()
    attended = jnp.concatenate([att[0], att[1]], axis=0).astype(jnp.bfloat16)

    def o_copy(step, source):
        return peer_copy(osend.at[step], oin.at[source], o_s.at[step], o_r.at[source], step)

    @pl.loop(1, gy)
    def _(step):
        load_out(step).wait()
        osend[step] = jnp.dot(
            attended, wo_v[step], preferred_element_type=jnp.float32
        ).astype(jnp.bfloat16)
        o_copy(step, me).start()

    load_out(0).wait()
    result = jnp.dot(attended, wo_v[0], preferred_element_type=jnp.float32)
    for step in range(1, gy):
        source = (me + step) % gy
        o_copy(step, source).wait_recv()
        result = result + oin[source].astype(jnp.float32)
    out[...] = result.astype(out.dtype)

    swap.wait_send()
    att_swap.wait_send()
    for side in range(gx_count):
        for step in range(gy):
            if side or step:
                ssq_copy(side, step, my_id).wait_send()
    for step in range(1, gy):
        x_copy(step, me).wait_send()
        q_copy(step, me).wait_send()
        box_copy(step, me).wait_send()
        o_copy(step, me).wait_send()


def local(inputs, norm_gain, w_query, w_key, w_value, w_out, key_cache, value_cache, lengths):
    gy, gx_count = lax.axis_size("gy"), lax.axis_size("gx")
    rows, span, _ = key_cache.shape
    bd = inputs.shape[1]
    qw, ck = w_query.shape[1], w_key.shape[1]
    ow = w_out.shape[1] // gy
    hh = qw // HD
    hq = max(1, hh // KVH)
    nq = gy * hh // KVH
    bf16, f32 = jnp.bfloat16, jnp.float32

    gap = jnp.zeros((SUB - rows - 1, bd), bf16)
    end = jnp.zeros((SUB - rows, bd), bf16)
    packed = jnp.concatenate([inputs[:rows], norm_gain[None, :], gap, inputs[rows:], end], axis=0)

    vmem = pl.BlockSpec(memory_space=pltpu.VMEM)
    hbm = pl.BlockSpec(memory_space=pl.ANY)
    dma = pltpu.SemaphoreType.DMA
    scratch = [
        pltpu.VMEM((gy, 2 * SUB, bd), bf16),
        pltpu.VMEM((gx_count * gy, SUB, HD), f32),
        pltpu.VMEM((gy, bd, qw), bf16),
        pltpu.VMEM((gy, bd, ck), bf16),
        pltpu.VMEM((gy, bd, ck), bf16),
        pltpu.VMEM((gy, w_out.shape[0], ow), bf16),
        pltpu.VMEM(key_cache.shape, bf16),
        pltpu.VMEM(value_cache.shape, bf16),
        pltpu.VMEM((2, SUB, qw + 2 * HD), f32),
        pltpu.VMEM((2 * SUB, ck), f32),
        pltpu.VMEM((2 * SUB, ck), f32),
        pltpu.VMEM((SUB, qw + 2 * HD), f32),
        pltpu.VMEM((KVH, hq + 2, SUB, HD), f32),
        pltpu.VMEM((gy, hq + 2, SUB, HD), f32),
        pltpu.VMEM((nq, SUB, HD), f32),
        pltpu.VMEM((nq, 2, SUB, HD), f32),
        pltpu.VMEM((gy, hq, 2, SUB, HD), f32),
        pltpu.VMEM((2, SUB, qw), f32),
        pltpu.VMEM((gy, 2 * SUB, ow), bf16),
        pltpu.VMEM((gy, 2 * SUB, ow), bf16),
        dma((gy,)), dma((gy,)), dma((gy,)), dma((gy,)), dma((rows,)), dma((rows,)),
        dma((gx_count, gy)), dma((gx_count * gy,)),
        dma((gy,)), dma((gy,)),
        dma, dma,
        dma((gy,)), dma((gy,)),
        dma((gy,)), dma((gy,)),
        dma, dma,
        dma((gy,)), dma((gy,)),
    ]
    result = pl.pallas_call(
        functools.partial(block_kernel, gy, gx_count, rows),
        out_shape=jax.ShapeDtypeStruct((2 * SUB, ow), bf16),
        in_specs=[vmem, vmem] + [hbm] * 6,
        out_specs=vmem,
        scratch_shapes=scratch,
        compiler_params=pltpu.CompilerParams(
            collective_id=0, has_side_effects=True, vmem_limit_bytes=52 * 2**20
        ),
    )(rope_table(lengths), packed, w_query, w_key, w_value, w_out, key_cache, value_cache)
    return jnp.concatenate([result[:rows], result[SUB : SUB + rows]], axis=0)


def solution(mesh):
    placed = (
        P("groups", ("gx", "gy")),
        P(("gx", "gy")),
        P("gx", "gy"),
        P("gx", "gy"),
        P("gx", "gy"),
        P("gy", "gx"),
        P(("groups", "gx"), "gy", None),
        P(("groups", "gx"), "gy", None),
        P(("groups", "gx")),
    )
    return jax.shard_map(
        local, mesh=mesh, in_specs=placed, out_specs=P("groups", ("gx", "gy")), check_vma=False
    )
```

time: 304 us -> 48.1 us (0.16)
  blocking collectives: 157 us -> 0 us
  waiting for transfers between devices: 73 us -> 0 us
  Pallas kernels: 0 us -> 39.5 us
  matrix products: 23.9 us -> 0 us
  between operations: 14.9 us -> 0.03 us
  starting transfers between devices: 14.2 us -> 0 us
  local copies, waits for them, and re-layouts: 14.5 us -> 6.16 us
  other arithmetic: 4.91 us -> 1.58 us
    all_gather x6 -> x0, blocking collectives: 148 us -> none  [the longest x1 32.9 us: local(): lax.all_gather(inputs, 'gy', axis=1, tiled=True)]
    reduce_scatter x1 -> x0, waiting for transfers between devices: 59.9 us -> none  [local(): lax.psum_scatter(partial_out.astype(jnp.bfloat16), 'gy', scatter_dimensio...]
    pallas_call x0 -> x1, Pallas kernels: none -> 39.5 us  [local(): pl.pallas_call(functools.partial(block_kernel, gy, gx_count, rows), out_s...]
    dot_general x6 -> x0, matrix products: 23.9 us -> none  [the longest x1 8.76 us: local(): jnp.dot(lax.all_gather(attended, 'gx', axis=0, tiled=True), w_out, prefer...]
    all_to_all x3 -> x0, waiting for transfers between devices: 13.1 us -> none  [the longest x1 7.49 us: local(): lax.all_to_all(send_weighted, 'gy', split_axis=0, concat_axis=0, tiled=True)]
    all_to_all x3 -> x0, starting transfers between devices: 11.3 us -> none  [the longest x1 4.63 us: local(): lax.all_to_all(send_weighted, 'gy', split_axis=0, concat_axis=0, tiled=True)]
    unnamed x2 -> x0, blocking collectives: 6.75 us -> none
    dynamic_update_slice x3 -> x0, local copies, waits for them, and re-layouts: 4.65 us -> none  [spread_heads(): lax.dynamic_update_slice_in_dim(filled, values[:, :, None], group_index, 2)]
  transfers between devices with their start and end apart: 5 -> 0, of which waited for: 4 -> 0; matrix products, arithmetic and copies ran while one was open for 6% -> 0% of each run, Pallas kernels for 0% -> 0%
where the time goes in v1:
time: 48.1 us; the launch traced here: 47.3 us
  Pallas kernels  39.5 us (82%)
  local copies, waits for them, and re-layouts  6.16 us (13%)
  other arithmetic  1.58 us (3%)
    pallas_call x1, Pallas kernels, local(): pl.pallas_call(functools.partial(block_kernel, gy, gx_count, rows), out_s...  39.5 us
    unnamed x4, local copies, waits for them, and re-layouts  4.53 us

profile of v1, /device:TPU:0, one launch (start us, length us, event | category | flops | bytes accessed | tf_op | source)
XLA Modules:
  0.0 47.3 jit_solution(13554089559443260643)
XLA Ops:
  0.0 0.0 copy-start
  0.0 0.7 %convert_element_type.5 = f32[6]{0:T(128)S(1)} convert(s32[6]{0:T(128)} %param.17) | non-fusion elementwise | flops 6 | bytes 48 | tf_op jit(solution)/shard_map/convert_element_type | solution.py:21
  0.8 0.1 stack_broadcast_in_dim.2
  0.8 0.7 %broadcast_in_dim.12 = bf16[1,1024]{1,0:T(2,128)(2,1)S(1)} reshape(bf16[1024]{0:T(1024)(128)(2,1)} %param.10) | data formatting | bytes 4096 | tf_op jit(solution)/shard_map/broadcast_in_dim | solution.py:342
  1.5 0.1 multiply_cosine_fusion
  1.6 0.1 maximum_bitcast_fusion
  1.7 0.8 %fusion.2 = (bf16[6,1024]{1,0:T(8,128)(2,1)S(1)}, bf16[6,1024]{1,0:T(8,128)(2,1)S(1)}) fusion(bf16[12,1024]{1,0:T(8,128)(2,1)} %param.9), kind=kLoop, calls=%fused_computation.11 | loop fusion | bytes 49152 | tf_op jit(solution)/shard_map/slice | solution.py:342
  2.5 0.1 concatenate.14.xp
  2.6 2.8 %copy.10.wk = bf16[8192,64]{1,0:T(8,128)(2,1)} copy(bf16[8192,64]{0,1:T(8,128)(2,1)} %param.12) | data formatting | bytes 2097152 | tf_op args[3]
  5.4 0.0 copy-done
  5.4 1.8 %copy.11.wv = bf16[8192,64]{1,0:T(8,128)(2,1)} copy(bf16[8192,64]{0,1:T(8,128)(2,1)S(1)} %copy-done) | data formatting | bytes 2097152 | tf_op args[4]
  7.1 39.5 %shard_map.91 = bf16[16,1024]{1,0:T(8,128)(2,1)S(1)} custom-call(f32[3,8,128]{2,1,0:T(8,128)S(1)} %select_maximum_fusion.table, bf16[16,1024]{1,0:T(8,128)(2,1)S(1)} %concatenate.14.xp, bf16[8192,1024]{1,0:T(8,128)(2,1)} %wq.1, bf16[8192,64]{1,0:T(8,128)(2,1)} %copy.10.wk, bf16[8192,64]{1,0:T(8,128)(2,1)} %copy.11.wv, bf16[1024,8192]{1,0:T(8,128)(2,1)} %wo.1, ...), custom_call_target="tpu_custom_call" | custom-call | tf_op jit(solution)/shard_map/pallas_call | solution.py:377
  46.7 0.6 %pad_maximum_fusion = bf16[12,1024]{1,0:T(8,128)(2,1)} fusion(bf16[6,1024]{1,0:T(8,128)(2,1)S(1)} %get-tuple-element.6, bf16[6,1024]{1,0:T(8,128)(2,1)S(1)} %get-tuple-element.5), kind=kLoop, calls=%fused_computation | loop fusion | flops 49152 | bytes 49152 | tf_op jit(solution)/shard_map/concatenate | solution.py:387
  (5 shorter events, 0.0 us)
Async XLA Ops:
  0.0 5.4 %copy-start = (bf16[8192,64]{0,1:T(8,128)(2,1)S(1)}, bf16[8192,64]{0,1:T(8,128)(2,1)}, u32[]{:S(2)}) copy-start(bf16[8192,64]{0,1:T(8,128)(2,1)} %param.13) | copy-start | bytes 3145732

commit v2 on v1

--- a/solution.py
+++ b/solution.py
@@ -2,6 +2,7 @@
 
 import jax
 import jax.numpy as jnp
+import numpy as np
 from jax import lax
 from jax.experimental import pallas as pl
 from jax.experimental.pallas import tpu as pltpu
@@ -14,26 +15,9 @@
 MESH = pl.DeviceIdType.MESH
 
 
-def rope_table(lengths):
-    half_dim = HD // 2
-    freq_index = jnp.arange(half_dim, dtype=jnp.float32)
-    inverse = 500000.0 ** (-2.0 * freq_index / HD)
-    floats = lengths.astype(jnp.float32)
-    angles = floats[:, None] * inverse[None, :]
-    cosine, sine = jnp.cos(angles), jnp.sin(angles)
-    table = jnp.stack(
-        [
-            jnp.concatenate([cosine, cosine], axis=1),
-            jnp.concatenate([-sine, sine], axis=1),
-            jnp.broadcast_to(floats[:, None], (lengths.shape[0], HD)),
-        ]
-    )
-    return jnp.pad(table, ((0, 0), (0, SUB - lengths.shape[0]), (0, 0)))
-
-
 def block_kernel(
     gy, gx_count, rows,
-    table, xp, wq, wk, wv, wo, kc, vc,
+    lengths, inverse, x, gain, wq, wk, wv, wo, kc, vc,
     out,
     xall, ssq, wq_v, wk_v, wv_v, wo_v, kc_v, vc_v,
     part, kpart, vpart, part_in, qsend, qin, qg, outbox, inbox, att, osend, oin,
@@ -43,9 +27,9 @@
     gx = lax.axis_index("gx")
     me = lax.axis_index("gy")
     other = 1 - gx
-    bd = xp.shape[1]
+    bd = x.shape[1]
     qw = wq.shape[1]
-    ck = wk.shape[1]
+    ck = wk.shape[0]
     span = kc.shape[1]
     ow = wo.shape[1] // gy
     hh = qw // HD
@@ -61,8 +45,8 @@
         rows_here = pl.ds(base, bd)
         return (
             pltpu.make_async_copy(wq.at[rows_here, :], wq_v.at[step], sem_wq.at[step]),
-            pltpu.make_async_copy(wk.at[rows_here, :], wk_v.at[step], sem_wk.at[step]),
-            pltpu.make_async_copy(wv.at[rows_here, :], wv_v.at[step], sem_wv.at[step]),
+            pltpu.make_async_copy(wk.at[:, rows_here], wk_v.at[step], sem_wk.at[step]),
+            pltpu.make_async_copy(wv.at[:, rows_here], wv_v.at[step], sem_wv.at[step]),
         )
 
     def load_out(step):
@@ -90,7 +74,14 @@
                 device_id_type=MESH,
             )
 
-    mine = xp[...].astype(jnp.float32)
+    own = x[...].astype(jnp.float32)
+    mine = jnp.concatenate(
+        [
+            own[:rows], gain[...].astype(jnp.float32), jnp.zeros((SUB - rows - 1, bd), jnp.float32),
+            own[rows:], jnp.zeros((SUB - rows, bd), jnp.float32),
+        ],
+        axis=0,
+    )
     diagonal = lax.broadcasted_iota(jnp.int32, (2 * SUB, HD), 0) == lax.broadcasted_iota(
         jnp.int32, (2 * SUB, HD), 1
     )
@@ -99,7 +90,7 @@
     ssq[my_id] = jnp.broadcast_to(
         jnp.sum(jnp.where(diagonal, squares, 0.0), axis=0, keepdims=True), (SUB, HD)
     )
-    xall[me] = xp[...]
+    xall[me] = mine.astype(jnp.bfloat16)
 
     pl.semaphore_wait(barrier, gx_count * gy - 1)
 
@@ -124,7 +115,7 @@
         )
 
     def x_copy(step, source):
-        return peer_copy(xp, xall.at[source], x_s.at[step], x_r.at[source], step)
+        return peer_copy(xall.at[me], xall.at[source], x_s.at[step], x_r.at[source], step)
 
     for side in range(gx_count):
         for step in range(gy):
@@ -139,6 +130,15 @@
     part[...] = jnp.zeros_like(part)
     kpart[...] = jnp.zeros_like(kpart)
     vpart[...] = jnp.zeros_like(vpart)
+    row_of = lax.broadcasted_iota(jnp.int32, (SUB, HD), 0)
+    lens = jnp.zeros((SUB, HD), jnp.int32)
+    for row in range(rows):
+        lens = jnp.where(row_of == row, lengths[row], lens)
+    lens = lens.astype(jnp.float32)
+    angles = lens * inverse[...]
+    cosine = jnp.cos(angles)
+    sine = jnp.sin(angles)
+    sine = jnp.where(lax.broadcasted_iota(jnp.int32, (SUB, HD), 1) < HD // 2, -sine, sine)
     outbox[...] = jnp.zeros_like(outbox)
 
     for side in range(gx_count):
@@ -160,8 +160,13 @@
         query = jnp.dot(normed, wq_v[step], preferred_element_type=jnp.float32)
         part[0, :, :qw] += query[:SUB]
         part[1, :, :qw] += query[SUB:]
-        kpart[...] += jnp.dot(normed, wk_v[step], preferred_element_type=jnp.float32)
-        vpart[...] += jnp.dot(normed, wv_v[step], preferred_element_type=jnp.float32)
+        across = (((1,), (1,)), ((), ()))
+        kpart[...] += lax.dot_general(
+            normed, wk_v[step], across, preferred_element_type=jnp.float32
+        )
+        vpart[...] += lax.dot_general(
+            normed, wv_v[step], across, preferred_element_type=jnp.float32
+        )
 
     project(0)
 
@@ -183,7 +188,6 @@
     target = lax.broadcasted_iota(jnp.int32, (HD, KVH * HD), 1)
     wanted = (target % HD) * KVH + target // HD
     select = jnp.where((column < ck) & (column + me * ck == wanted), 1.0, 0.0).astype(jnp.bfloat16)
-    cosine, sine, lens = table[0], table[1], table[2]
     swap.wait_recv()
 
     def rotated(values):
@@ -337,9 +341,9 @@
     nq = gy * hh // KVH
     bf16, f32 = jnp.bfloat16, jnp.float32
 
-    gap = jnp.zeros((SUB - rows - 1, bd), bf16)
-    end = jnp.zeros((SUB - rows, bd), bf16)
-    packed = jnp.concatenate([inputs[:rows], norm_gain[None, :], gap, inputs[rows:], end], axis=0)
+    half_dim = HD // 2
+    inverse = 500000.0 ** (-2.0 * np.arange(half_dim, dtype=np.float64) / HD)
+    inverse = jnp.asarray(np.tile(inverse, 2)[None, :], f32)
 
     vmem = pl.BlockSpec(memory_space=pltpu.VMEM)
     hbm = pl.BlockSpec(memory_space=pl.ANY)
@@ -348,8 +352,8 @@
         pltpu.VMEM((gy, 2 * SUB, bd), bf16),
         pltpu.VMEM((gx_count * gy, SUB, HD), f32),
         pltpu.VMEM((gy, bd, qw), bf16),
-        pltpu.VMEM((gy, bd, ck), bf16),
-        pltpu.VMEM((gy, bd, ck), bf16),
+        pltpu.VMEM((gy, ck, bd), bf16),
+        pltpu.VMEM((gy, ck, bd), bf16),
         pltpu.VMEM((gy, w_out.shape[0], ow), bf16),
         pltpu.VMEM(key_cache.shape, bf16),
         pltpu.VMEM(value_cache.shape, bf16),
@@ -377,13 +381,16 @@
     result = pl.pallas_call(
         functools.partial(block_kernel, gy, gx_count, rows),
         out_shape=jax.ShapeDtypeStruct((2 * SUB, ow), bf16),
-        in_specs=[vmem, vmem] + [hbm] * 6,
+        in_specs=[pl.BlockSpec(memory_space=pltpu.SMEM)] + [vmem] * 3 + [hbm] * 6,
         out_specs=vmem,
         scratch_shapes=scratch,
         compiler_params=pltpu.CompilerParams(
-            collective_id=0, has_side_effects=True, vmem_limit_bytes=52 * 2**20
+            collective_id=0, has_side_effects=True, vmem_limit_bytes=60 * 2**20
         ),
-    )(rope_table(lengths), packed, w_query, w_key, w_value, w_out, key_cache, value_cache)
+    )(
+        lengths, inverse, inputs, norm_gain[None, :],
+        w_query, w_key.T, w_value.T, w_out, key_cache, value_cache,
+    )
     return jnp.concatenate([result[:rows], result[SUB : SUB + rows]], axis=0)
 
 

time: 48.1 us -> 44.4 us (0.923)
  local copies, waits for them, and re-layouts: 6.16 us -> 2.02 us
  Pallas kernels: 39.5 us -> 41 us
  other arithmetic: 1.58 us -> 0.63 us
    unnamed x4 -> x0, local copies, waits for them, and re-layouts: 4.53 us -> none
    pallas_call x1, Pallas kernels: 39.5 us -> 41 us  [local(): pl.pallas_call(functools.partial(block_kernel, gy, gx_count, rows), out_s...]
    slice x1 -> x0, local copies, waits for them, and re-layouts: 0.81 us -> none  [local(): inputs[rows:]]
    convert_element_type x1 -> x0, other arithmetic: 0.75 us -> none  [rope_table(): floats = lengths.astype(jnp.float32)]
    slice x1, local copies, waits for them, and re-layouts: 0.01 us -> 0.74 us  [local(): return jnp.concatenate([result[:rows], result[SUB:SUB + rows]], axis=0)]
    broadcast_in_dim x1, local copies, waits for them, and re-layouts: 0.69 us -> 1.28 us  [local(): norm_gain[None, :]]
where the time goes in v2:
time: 44.4 us; the launch traced here: 43.6 us
  Pallas kernels  41 us (92%)
  local copies, waits for them, and re-layouts  2.02 us (5%)
  other arithmetic  0.63 us (1%)
    pallas_call x1, Pallas kernels, local(): pl.pallas_call(functools.partial(block_kernel, gy, gx_count, rows), out_s...  41 us
    broadcast_in_dim x1, local copies, waits for them, and re-layouts, local(): norm_gain[None, :]  1.28 us

profile of v2, /device:TPU:0, one launch (start us, length us, event | category | flops | bytes accessed | tf_op | source)
XLA Modules:
  0.0 43.6 jit_solution(18071542294260511140)
XLA Ops:
  0.0 1.3 %broadcast_in_dim.3.gain = bf16[1,1024]{1,0:T(2,128)(2,1)} reshape(bf16[1024]{0:T(1024)(128)(2,1)} %param.11) | data formatting | bytes 4096 | tf_op jit(solution)/shard_map/broadcast_in_dim | solution.py:391
  1.3 41.0 %shard_map.100 = bf16[16,1024]{1,0:T(8,128)(2,1)} custom-call(s32[6]{0:T(128)} %lengths.1, f32[1,128]{1,0:T(1,128)} %constant.2.clone.inverse, bf16[12,1024]{1,0:T(8,128)(2,1)} %x.1, bf16[1,1024]{1,0:T(2,128)(2,1)} %broadcast_in_dim.3.gain, bf16[8192,1024]{1,0:T(8,128)(2,1)} %wq.1, bf16[64,8192]{1,0:T(8,128)(2,1)} %bitcast.2, bf16[64,8192]{1,0:T(8,128)(2,1)} %bitcast.3, ...), custom_call_target="tpu_custom_call" | custom-call | tf_op jit(solution)/shard_map/pallas_call | solution.py:381
  42.2 0.7 %fusion = (bf16[6,1024]{1,0:T(8,128)(2,1)S(1)}, bf16[6,1024]{1,0:T(8,128)(2,1)S(1)}) fusion(bf16[16,1024]{1,0:T(8,128)(2,1)} %shard_map.100), kind=kLoop, calls=%fused_computation.1 | loop fusion | bytes 49152 | tf_op jit(solution)/shard_map/slice | solution.py:394
  43.0 0.6 %pad_maximum_fusion = bf16[12,1024]{1,0:T(8,128)(2,1)} fusion(bf16[6,1024]{1,0:T(8,128)(2,1)S(1)} %get-tuple-element.6, bf16[6,1024]{1,0:T(8,128)(2,1)S(1)} %get-tuple-element.5), kind=kLoop, calls=%fused_computation | loop fusion | flops 49152 | bytes 49152 | tf_op jit(solution)/shard_map/concatenate | solution.py:394

commit v3 on v2

--- a/solution.py
+++ b/solution.py
@@ -20,13 +20,17 @@
     lengths, inverse, x, gain, wq, wk, wv, wo, kc, vc,
     out,
     xall, ssq, wq_v, wk_v, wv_v, wo_v, kc_v, vc_v,
-    part, kpart, vpart, part_in, qsend, qin, qg, outbox, inbox, att, osend, oin,
+    part, kpart, vpart, part_in, qtile, qsend, qin, kvsend, kvin, qg,
+    sums, box, box_in, stat, stat_in, att, osend, pin, oin,
     sem_wq, sem_wk, sem_wv, sem_wo, sem_kc, sem_vc,
-    ssq_s, ssq_r, x_s, x_r, part_s, part_r, q_s, q_r, box_s, box_r, att_s, att_r, o_s, o_r,
+    ssq_s, ssq_r, x_s, x_f, x_r, part_s, part_r, q_s, q_r, kv_s, kv_r,
+    box_s, box_r, stat_s, stat_r, att_s, att_r, p_s, p_r, o_s, o_r,
 ):
     gx = lax.axis_index("gx")
     me = lax.axis_index("gy")
     other = 1 - gx
+    half = gy // 2
+    mate = me + 1 - 2 * (me % 2)
     bd = x.shape[1]
     qw = wq.shape[1]
     ck = wk.shape[0]
@@ -38,10 +42,15 @@
     bph = gy // KVH
     group = me // bph
     block = me % bph
+    cj = ck // KVH
+    qm = qsend.shape[1]
     d_model = bd * gy * gx_count
 
+    def block_at(step):
+        return (me + (step // half) * (mate - me) + 2 * (step % half)) % gy
+
     def load_in(step):
-        base = pl.multiple_of(((me + step) % gy) * bd, bd)
+        base = pl.multiple_of(block_at(step) * bd, bd)
         rows_here = pl.ds(base, bd)
         return (
             pltpu.make_async_copy(wq.at[rows_here, :], wq_v.at[step], sem_wq.at[step]),
@@ -50,7 +59,8 @@
         )
 
     def load_out(step):
-        base = pl.multiple_of(((me + step) % gy) * ow, ow)
+        first = mate + (step // half) * (me - mate)
+        base = pl.multiple_of(((first + 2 * ((step + 1) % half)) % gy) * ow, ow)
         return pltpu.make_async_copy(wo.at[:, pl.ds(base, ow)], wo_v.at[step], sem_wo.at[step])
 
     def load_cache(row):
@@ -114,15 +124,29 @@
             device_id={"gx": other}, device_id_type=MESH,
         )
 
-    def x_copy(step, source):
-        return peer_copy(xall.at[me], xall.at[source], x_s.at[step], x_r.at[source], step)
+    def gy_copy(src, dst, send, recv, device):
+        return pltpu.make_async_remote_copy(
+            src_ref=src, dst_ref=dst, send_sem=send, recv_sem=recv,
+            device_id={"gy": device}, device_id_type=MESH,
+        )
+
+    def x_copy(k, source):
+        device = mate if k == 0 else (me + 2 * k) % gy
+        return gy_copy(xall.at[me], xall.at[source], x_s.at[k], x_r.at[source], device)
+
+    def x_forward(k):
+        passed = (me + 2 * k) % gy
+        return gy_copy(xall.at[passed], xall.at[passed], x_f.at[k], x_r.at[passed], mate)
+
+    def x_wait(source):
+        gy_copy(xall.at[me], xall.at[source], x_s.at[0], x_r.at[source], mate).wait_recv()
 
     for side in range(gx_count):
         for step in range(gy):
             if side or step:
                 ssq_copy(side, step, my_id).start()
-    for step in range(1, gy):
-        x_copy(step, me).start()
+    for k in list(range(1, half)) + [0]:
+        x_copy(k, me).start()
     for row in range(rows):
         for copy in load_cache(row):
             copy.start()
@@ -139,7 +163,11 @@
     cosine = jnp.cos(angles)
     sine = jnp.sin(angles)
     sine = jnp.where(lax.broadcasted_iota(jnp.int32, (SUB, HD), 1) < HD // 2, -sine, sine)
-    outbox[...] = jnp.zeros_like(outbox)
+    sums[...] = jnp.zeros_like(sums)
+    qtile[...] = jnp.zeros_like(qtile)
+    for k in range(1, half):
+        x_wait((me + 2 * k) % gy)
+        x_forward(k).start()
 
     for side in range(gx_count):
         for step in range(gy):
@@ -151,8 +179,7 @@
     scale_inv = lax.rsqrt(total / d_model + 1e-05)
 
     def project(step):
-        source = (me + step) % gy
-        features = xall[source].astype(jnp.float32)
+        features = xall[block_at(step)].astype(jnp.float32)
         gain = features[rows : rows + 1, :]
         normed = (features * scale_inv * gain).astype(jnp.bfloat16)
         for copy in load_in(step):
@@ -168,12 +195,13 @@
             normed, wv_v[step], across, preferred_element_type=jnp.float32
         )
 
-    project(0)
-
-    @pl.loop(1, gy)
+    @pl.loop(0, half)
     def _(step):
-        source = (me + step) % gy
-        x_copy(step, source).wait_recv()
+        project(step)
+
+    @pl.loop(half, gy)
+    def _(step):
+        x_wait(block_at(step))
         project(step)
 
     for side in range(2):
@@ -183,11 +211,11 @@
     swap = core_copy(part.at[other], part_in, part_s, part_r)
     swap.start()
     for step in range(gy):
-        load_out((step + 1) % gy).start()
+        load_out(step).start()
     column = lax.broadcasted_iota(jnp.int32, (HD, KVH * HD), 0)
     target = lax.broadcasted_iota(jnp.int32, (HD, KVH * HD), 1)
     wanted = (target % HD) * KVH + target // HD
-    select = jnp.where((column < ck) & (column + me * ck == wanted), 1.0, 0.0).astype(jnp.bfloat16)
+    select = jnp.where((column < ck) & (column == wanted), 1.0, 0.0).astype(jnp.bfloat16)
     swap.wait_recv()
 
     def rotated(values):
@@ -197,7 +225,9 @@
     for slot in range(hh):
         turned = rotated(summed[:, slot * HD : (slot + 1) * HD])
         to_group = slot % KVH if hh % KVH == 0 else (me * hh + slot) % KVH
-        qsend[to_group, slot // KVH] = turned.astype(jnp.bfloat16).astype(jnp.float32)
+        at = slot // KVH * SUB
+        qtile[to_group, at : at + SUB] = turned
+    qsend[...] = qtile[...].astype(jnp.bfloat16)
     pair = jnp.concatenate([summed[:, qw : qw + HD], summed[:, qw + HD :]], axis=0)
     high = pair.astype(jnp.bfloat16)
     rest = pair - high.astype(jnp.float32)
@@ -209,33 +239,50 @@
         + jnp.dot(low, select, preferred_element_type=jnp.float32)
     )
     for g in range(KVH):
-        qsend[g, hq] = placed[:SUB, g * HD : (g + 1) * HD]
-        qsend[g, hq + 1] = placed[SUB:, g * HD : (g + 1) * HD]
-
-    def q_copy(step, source):
-        return peer_copy(
-            qsend.at[((me + step) % gy) // bph], qin.at[source],
-            q_s.at[step], q_r.at[source], step,
+        lanes = slice(g * HD, (g + 1) * HD)
+        kvsend[g] = placed[:SUB, lanes] + pltpu.roll(placed[SUB:, lanes], HD // 2, 1)
+
+    def q_copies(step, source):
+        to_group = ((me + step) % gy) // bph
+        return (
+            peer_copy(qsend.at[to_group], qin.at[source], q_s.at[step], q_r.at[source], step),
+            peer_copy(kvsend.at[to_group], kvin.at[source], kv_s.at[step], kv_r.at[source], step),
         )
 
     for step in range(1, gy):
-        q_copy(step, me).start()
+        for copy in q_copies(step, me):
+            copy.start()
     qin[me] = qsend[group]
+    kvin[me] = kvsend[group]
     for step in range(1, gy):
-        q_copy(step, (me + step) % gy).wait_recv()
-
-    for n in range(nq):
-        if hh % KVH == 0:
-            qg[n] = qin[n * KVH // hh, (n * KVH % hh) // KVH]
-        else:
-            qg[n] = qin[(n * KVH + group) // hh, 0]
-    own_key = rotated(jnp.sum(qin[:, hq], axis=0)).astype(jnp.bfloat16).astype(jnp.float32)
-    own_value = jnp.sum(qin[:, hq + 1], axis=0).astype(jnp.bfloat16).astype(jnp.float32)
+        for copy in q_copies(step, (me + step) % gy):
+            copy.wait_recv()
+
+    if hh % KVH == 0:
+        for source in range(gy):
+            tile = qin[source].astype(jnp.float32)
+            for slot in range(hq):
+                qg[source * hq + slot] = tile[slot * SUB : (slot + 1) * SUB]
+    else:
+        for n in range(nq):
+            qg[n] = qin[(n * KVH + group) // hh].astype(jnp.float32)[:SUB]
+    lane8 = lax.broadcasted_iota(jnp.int32, (SUB, HD), 1)
+    own_key = jnp.zeros((SUB, HD), jnp.float32)
+    own_value = jnp.zeros((SUB, HD), jnp.float32)
+    for source in range(gy):
+        tile = kvin[source]
+        key_lanes = jnp.where(lane8 < HD // 2, tile, 0.0)
+        value_lanes = jnp.where(lane8 < HD // 2, 0.0, tile)
+        own_key += pltpu.roll(key_lanes, source * cj, 1) if source else key_lanes
+        own_value += pltpu.roll(value_lanes, (source * cj + HD // 2) % HD, 1)
+    own_key = rotated(own_key).astype(jnp.bfloat16).astype(jnp.float32)
+    own_value = own_value.astype(jnp.bfloat16).astype(jnp.float32)
 
     score_scale = HD ** (-0.5)
     with_self = (lax.broadcasted_iota(jnp.int32, (nq, 1), 0) * 0 + block) == 0
     positions = (lax.broadcasted_iota(jnp.int32, (nq, span), 1) + block * span).astype(jnp.float32)
     lane = lax.broadcasted_iota(jnp.int32, (nq, HD), 1)
+    stats = jnp.zeros((nq, HD), jnp.float32)
     for row in range(rows):
         for copy in load_cache(row):
             copy.wait()
@@ -264,31 +311,53 @@
             weighted
             + self_weight.astype(jnp.bfloat16).astype(jnp.float32) * own_value[row : row + 1, :]
         )
-        outbox[:, 0, row, :] = weighted
-        outbox[:, 1, row, :] = jnp.where(lane < HD // 2, best, denominator)
-
-    def box_copy(step, source):
-        first = (((me + step) % gy) * hh) // KVH
-        return peer_copy(
-            outbox.at[pl.ds(first, hq)], inbox.at[source], box_s.at[step], box_r.at[source], step
+        sums[:, row, :] = weighted
+        stats = jnp.where(lane == row, best, stats)
+        stats = jnp.where(lane == SUB + row, denominator, stats)
+
+    stat[...] = jnp.zeros_like(stat)
+    for owner in range(gy):
+        first = owner * hh // KVH
+        heads = [sums[first + slot] for slot in range(hq)]
+        heads += [jnp.zeros((SUB, HD), jnp.float32)] * (qm // SUB - hq)
+        box[owner] = jnp.concatenate(heads, axis=0).astype(jnp.bfloat16)
+        stat[owner, :hq] = stats[first : first + hq]
+
+    def box_copies(step, source):
+        owner = (me + step) % gy
+        return (
+            peer_copy(
+                stat.at[owner, pl.ds(0, hq)], stat_in.at[source, pl.ds(0, hq)],
+                stat_s.at[step], stat_r.at[source], step,
+            ),
+            peer_copy(box.at[owner], box_in.at[source], box_s.at[step], box_r.at[source], step),
         )
 
     for step in range(1, gy):
-        box_copy(step, me).start()
-    inbox[me] = outbox[pl.ds((me * hh) // KVH, hq)]
+        for copy in box_copies(step, me):
+            copy.start()
+    box_in[me] = box[me]
+    stat_in[me] = stat[me]
     for step in range(1, gy):
-        box_copy(step, (me + step) % gy).wait_recv()
+        for copy in box_copies(step, (me + step) % gy):
+            copy.wait_recv()
 
     for slot in range(hh):
         of_group = slot % KVH if hh % KVH == 0 else (me * hh + slot) % KVH
-        sums = [inbox[of_group * bph + b, slot // KVH, 0] for b in range(bph)]
-        stats = [inbox[of_group * bph + b, slot // KVH, 1] for b in range(bph)]
-        bests = [s[:, 0:1] for s in stats]
-        denominators = [s[:, HD // 2 : HD // 2 + 1] for s in stats]
+        at = slot // KVH
+        bests, denominators, parts = [], [], []
+        for b in range(bph):
+            source = of_group * bph + b
+            line = stat_in[source, at : at + 1, :]
+            bests.append(jnp.sum(jnp.where(lane8 == row_of, line, 0.0), axis=1, keepdims=True))
+            denominators.append(
+                jnp.sum(jnp.where(lane8 == row_of + SUB, line, 0.0), axis=1, keepdims=True)
+            )
+            parts.append(box_in[source].astype(jnp.float32)[at * SUB : (at + 1) * SUB])
         overall = functools.reduce(jnp.maximum, bests)
-        factors = [jnp.exp(b - overall) for b in bests]
+        factors = [jnp.exp(best - overall) for best in bests]
         denominator = sum(f * d for f, d in zip(factors, denominators))
-        weighted = sum(f * s for f, s in zip(factors, sums))
+        weighted = sum(f * p for f, p in zip(factors, parts))
         att[gx, :, slot * HD : (slot + 1) * HD] = (
             (weighted / denominator).astype(jnp.bfloat16).astype(jnp.float32)
         )
@@ -298,24 +367,42 @@
     core_copy(att.at[other], att.at[other], att_s, att_r).wait_recv()
     attended = jnp.concatenate([att[0], att[1]], axis=0).astype(jnp.bfloat16)
 
-    def o_copy(step, source):
-        return peer_copy(osend.at[step], oin.at[source], o_s.at[step], o_r.at[source], step)
-
-    @pl.loop(1, gy)
+    def p_copy(k):
+        return gy_copy(osend.at[k], pin.at[k], p_s.at[k], p_r.at[k], mate)
+
+    def o_copy(k, source):
+        return gy_copy(
+            osend.at[half + k], oin.at[source // 2], o_s.at[k], o_r.at[source // 2],
+            (me + 2 * k) % gy,
+        )
+
+    @pl.loop(0, half)
     def _(step):
+        k = (step + 1) % half
         load_out(step).wait()
-        osend[step] = jnp.dot(
+        osend[k] = jnp.dot(
             attended, wo_v[step], preferred_element_type=jnp.float32
         ).astype(jnp.bfloat16)
-        o_copy(step, me).start()
-
-    load_out(0).wait()
-    result = jnp.dot(attended, wo_v[0], preferred_element_type=jnp.float32)
-    for step in range(1, gy):
-        source = (me + step) % gy
-        o_copy(step, source).wait_recv()
-        result = result + oin[source].astype(jnp.float32)
-    out[...] = result.astype(out.dtype)
+        p_copy(k).start()
+
+    @pl.loop(half, gy - 1)
+    def _(step):
+        k = step + 1 - half
+        load_out(step).wait()
+        share = jnp.dot(attended, wo_v[step], preferred_element_type=jnp.float32)
+        p_copy(k).wait_recv()
+        osend[half + k] = (share + pin[k].astype(jnp.float32)).astype(jnp.bfloat16)
+        o_copy(k, me).start()
+
+    load_out(gy - 1).wait()
+    result = jnp.dot(attended, wo_v[gy - 1], preferred_element_type=jnp.float32)
+    p_copy(0).wait_recv()
+    result = result + pin[0].astype(jnp.float32)
+    for k in range(1, half):
+        source = (me + 2 * k) % gy
+        o_copy(k, source).wait_recv()
+        result = result + oin[source // 2].astype(jnp.float32)
+    out[...] = jnp.concatenate([result[:rows], result[SUB : SUB + rows]], axis=0).astype(out.dtype)
 
     swap.wait_send()
     att_swap.wait_send()
@@ -323,11 +410,15 @@
         for step in range(gy):
             if side or step:
                 ssq_copy(side, step, my_id).wait_send()
+    for k in range(half):
+        x_copy(k, me).wait_send()
+        p_copy(k).wait_send()
+        if k:
+            x_forward(k).wait_send()
+            o_copy(k, me).wait_send()
     for step in range(1, gy):
-        x_copy(step, me).wait_send()
-        q_copy(step, me).wait_send()
-        box_copy(step, me).wait_send()
-        o_copy(step, me).wait_send()
+        for copy in q_copies(step, me) + box_copies(step, me):
+            copy.wait_send()
 
 
 def local(inputs, norm_gain, w_query, w_key, w_value, w_out, key_cache, value_cache, lengths):
@@ -339,6 +430,8 @@
     hh = qw // HD
     hq = max(1, hh // KVH)
     nq = gy * hh // KVH
+    half = gy // 2
+    qm = max(2 * SUB, hq * SUB)
     bf16, f32 = jnp.bfloat16, jnp.float32
 
     half_dim = HD // 2
@@ -361,26 +454,33 @@
         pltpu.VMEM((2 * SUB, ck), f32),
         pltpu.VMEM((2 * SUB, ck), f32),
         pltpu.VMEM((SUB, qw + 2 * HD), f32),
-        pltpu.VMEM((KVH, hq + 2, SUB, HD), f32),
-        pltpu.VMEM((gy, hq + 2, SUB, HD), f32),
+        pltpu.VMEM((KVH, qm, HD), f32),
+        pltpu.VMEM((KVH, qm, HD), bf16),
+        pltpu.VMEM((gy, qm, HD), bf16),
+        pltpu.VMEM((KVH, SUB, HD), f32),
+        pltpu.VMEM((gy, SUB, HD), f32),
         pltpu.VMEM((nq, SUB, HD), f32),
-        pltpu.VMEM((nq, 2, SUB, HD), f32),
-        pltpu.VMEM((gy, hq, 2, SUB, HD), f32),
+        pltpu.VMEM((nq, SUB, HD), f32),
+        pltpu.VMEM((gy, qm, HD), bf16),
+        pltpu.VMEM((gy, qm, HD), bf16),
+        pltpu.VMEM((gy, SUB, HD), f32),
+        pltpu.VMEM((gy, SUB, HD), f32),
         pltpu.VMEM((2, SUB, qw), f32),
         pltpu.VMEM((gy, 2 * SUB, ow), bf16),
-        pltpu.VMEM((gy, 2 * SUB, ow), bf16),
+        pltpu.VMEM((half, 2 * SUB, ow), bf16),
+        pltpu.VMEM((half, 2 * SUB, ow), bf16),
         dma((gy,)), dma((gy,)), dma((gy,)), dma((gy,)), dma((rows,)), dma((rows,)),
         dma((gx_count, gy)), dma((gx_count * gy,)),
-        dma((gy,)), dma((gy,)),
+        dma((half,)), dma((half,)), dma((gy,)),
         dma, dma,
-        dma((gy,)), dma((gy,)),
-        dma((gy,)), dma((gy,)),
+        dma((gy,)), dma((gy,)), dma((gy,)), dma((gy,)),
+        dma((gy,)), dma((gy,)), dma((gy,)), dma((gy,)),
         dma, dma,
-        dma((gy,)), dma((gy,)),
+        dma((half,)), dma((half,)), dma((half,)), dma((half,)),
     ]
-    result = pl.pallas_call(
+    return pl.pallas_call(
         functools.partial(block_kernel, gy, gx_count, rows),
-        out_shape=jax.ShapeDtypeStruct((2 * SUB, ow), bf16),
+        out_shape=jax.ShapeDtypeStruct((2 * rows, ow), bf16),
         in_specs=[pl.BlockSpec(memory_space=pltpu.SMEM)] + [vmem] * 3 + [hbm] * 6,
         out_specs=vmem,
         scratch_shapes=scratch,
@@ -391,7 +491,6 @@
         lengths, inverse, inputs, norm_gain[None, :],
         w_query, w_key.T, w_value.T, w_out, key_cache, value_cache,
     )
-    return jnp.concatenate([result[:rows], result[SUB : SUB + rows]], axis=0)
 
 
 def solution(mesh):

time: 44.4 us -> 42.6 us (0.959); the launches traced: 43.6 us -> 42.4 us
  Pallas kernels: 41 us -> 39.7 us
  other arithmetic: 0.63 us -> 0 us
  local copies, waits for them, and re-layouts: 2.02 us -> 2.65 us
    unnamed x0 -> x1, local copies, waits for them, and re-layouts: none -> 1.38 us
    pallas_call x1, Pallas kernels: 41 us -> 39.7 us  [local(): pl.pallas_call(functools.partial(block_kernel, gy, gx_count, rows), out_s...]
    slice x1 -> x0, local copies, waits for them, and re-layouts: 0.74 us -> none  [local(): return jnp.concatenate([result[:rows], result[SUB:SUB + rows]], axis=0)]
    concatenate x1 -> x0, other arithmetic: 0.63 us -> none  [local(): return jnp.concatenate([result[:rows], result[SUB:SUB + rows]], axis=0)]
where the time goes in v3:
time: 42.6 us; the launch traced here: 42.4 us
  Pallas kernels  39.7 us (93%)
  local copies, waits for them, and re-layouts  2.65 us (6%)
    pallas_call x1, Pallas kernels, local(): pl.pallas_call(functools.partial(block_kernel, gy, gx_count, rows), out_s...  39.7 us
    unnamed x1, local copies, waits for them, and re-layouts  1.38 us
    broadcast_in_dim x1, local copies, waits for them, and re-layouts, local(): norm_gain[None, :]  1.28 us

profile of v3, /device:TPU:0, one launch (start us, length us, event | category | flops | bytes accessed | tf_op | source)
XLA Modules:
  0.0 42.4 jit_solution(4740154244512180462)
XLA Ops:
  0.0 1.3 %broadcast_in_dim.3.gain = bf16[1,1024]{1,0:T(2,128)(2,1)} reshape(bf16[1024]{0:T(1024)(128)(2,1)} %param.11) | data formatting | bytes 4096 | tf_op jit(solution)/shard_map/broadcast_in_dim | solution.py:491
  1.3 39.7 %shard_map.100 = bf16[12,1024]{1,0:T(8,128)(2,1)} custom-call(s32[6]{0:T(128)} %lengths.1, f32[1,128]{1,0:T(1,128)} %constant.2.clone.inverse, bf16[12,1024]{1,0:T(8,128)(2,1)} %x.1, bf16[1,1024]{1,0:T(2,128)(2,1)} %broadcast_in_dim.3.gain, bf16[8192,1024]{1,0:T(8,128)(2,1)} %wq.1, bf16[64,8192]{1,0:T(8,128)(2,1)} %bitcast.2, bf16[64,8192]{1,0:T(8,128)(2,1)} %bitcast.3, ...), custom_call_target="tpu_custom_call" | custom-call | tf_op jit(solution)/shard_map/pallas_call | solution.py:481
  41.0 1.4 %copy.12 = bf16[12,1024]{1,0:T(8,128)(2,1)} copy(bf16[12,1024]{1,0:T(8,128)(2,1)} %shard_map.100) | data formatting | bytes 49152
